TPU v7x, 256 devices: a whole 4x4x8 slice. The times are simulated.
256 devices in a mesh: patch: 64 (over y, z, core), sample: 4 (over x).
Axes of the slice: x: 4, y: 4, z: 8, core: 2. Of those that a mesh axis runs over, the one named last changes fastest.
Arguments:
- edge_latents: bfloat16 [4, 65536, 512], P('sample', 'patch'), may hold values from -6 to 6
- node_latents: bfloat16 [4, 16384, 512], P('sample', 'patch'), may hold values from -6 to 6
- edge_cotangent: bfloat16 [4, 65536, 512], P('sample', 'patch'), may hold values from -6 to 6
- node_cotangent: bfloat16 [4, 16384, 512], P('sample', 'patch'), may hold values from -6 to 6
- senders: int32 [65536], P('patch'), may hold values from 0 to 575, as said below
- receivers: int32 [65536], P('patch'), may hold values from 0 to 255
- send_rows: int32 [4096, 4], P('patch'), may hold values from 0 to 255
- edge_first: bfloat16 [1536, 512], replicated, may hold values from -0.15625 to 0.15625
- edge_second: bfloat16 [512, 512], replicated, may hold values from -0.25 to 0.25
- edge_gain: float32 [512], replicated, may hold values from 0.25 to 1.75
- node_first: bfloat16 [1024, 512], replicated, may hold values from -0.1875 to 0.1875
- node_second: bfloat16 [512, 512], replicated, may hold values from -0.25 to 0.25
- node_gain: float32 [512], replicated, may hold values from 0.25 to 1.75
Outputs:
- edge_grad: bfloat16 [4, 65536, 512], P('sample', 'patch')
- node_grad: bfloat16 [4, 16384, 512], P('sample', 'patch')
- edge_first_grad: bfloat16 [1536, 512], replicated
- edge_second_grad: bfloat16 [512, 512], replicated
- node_first_grad: bfloat16 [1024, 512], replicated
- node_second_grad: bfloat16 [512, 512], replicated
- edge_gain_grad: bfloat16 [512], replicated
- node_gain_grad: bfloat16 [512], replicated
Inputs may be any that keep to these rules, and one draw needn't show every extreme that they name: `senders`: each patch's sender table has 576 rows: the last 32 nodes of the patch before it (cyclically), its own 256 nodes, the first 32 nodes of the patch after it, then 4 rows from each patch in order.
All inputs are finite; a program needn't handle non-finite values.
Results may differ from a plain program's by a relative error of at most 0.012.
Values may be sent and summed in bfloat16 or wider, within the bound.
A program may use at most 128 MiB of HBM per device.

v0:
```python
import jax
import jax.numpy as jnp
from jax import lax
from jax.sharding import PartitionSpec as P

RIM = 32
FAR = 4


def with_halo(cells, sides, width):
    for axis, dim in sides:
        count = lax.axis_size(axis)
        head = lax.slice_in_dim(cells, 0, width, axis=dim)
        tail = lax.slice_in_dim(cells, cells.shape[dim] - width, cells.shape[dim], axis=dim)
        cells = jnp.concatenate(
            [
                lax.ppermute(tail, axis, [(i, (i + 1) % count) for i in range(count)]),
                cells,
                lax.ppermute(head, axis, [((i + 1) % count, i) for i in range(count)]),
            ],
            axis=dim,
        )
    return cells


def from_behind(array, axis, by):
    size = lax.axis_size(axis)
    return lax.ppermute(array, axis, [(i, (i + by) % size) for i in range(size)])


def normalize(values):
    center = values - jnp.mean(values, axis=1, keepdims=True)
    spread = jnp.mean(center * center, axis=1, keepdims=True)
    scale = lax.rsqrt(spread + 1e-05)
    return (center * scale, scale)


def normalize_back(grads, normed, scale):
    first = jnp.mean(grads, axis=1, keepdims=True)
    second = jnp.mean(grads * normed, axis=1, keepdims=True)
    return (grads - first - normed * second) * scale


def layer_backward(
    edges_in,
    sent_latent,
    nodes_in,
    recv_ids,
    edge_cot,
    node_cot,
    edge_first,
    edge_second,
    edge_gain,
    node_first,
    node_second,
    node_gain,
):
    width = nodes_in.shape[1]
    recv_latent = nodes_in[recv_ids]
    edge_input = jnp.concatenate([edges_in, sent_latent, recv_latent], axis=1)
    edge_pre = jnp.dot(edge_input, edge_first, preferred_element_type=jnp.float32)
    edge_sig = jax.nn.sigmoid(edge_pre)
    edge_act = (edge_pre * edge_sig).astype(jnp.bfloat16)
    edge_raw = jnp.dot(edge_act, edge_second, preferred_element_type=jnp.float32)
    edge_hat, edge_scale = normalize(edge_raw)
    update = edge_hat * edge_gain
    inflow = jax.ops.segment_sum(update, recv_ids, num_segments=nodes_in.shape[0]).astype(
        jnp.bfloat16
    )
    node_input = jnp.concatenate([nodes_in, inflow], axis=1)
    node_pre = jnp.dot(node_input, node_first, preferred_element_type=jnp.float32)
    node_sig = jax.nn.sigmoid(node_pre)
    node_act = (node_pre * node_sig).astype(jnp.bfloat16)
    node_raw = jnp.dot(node_act, node_second, preferred_element_type=jnp.float32)
    node_hat, node_scale = normalize(node_raw)
    node_upstream = node_cot.astype(jnp.float32)
    node_gain_grad = jnp.sum(node_upstream * node_hat, axis=0)
    node_raw_grad = normalize_back(node_upstream * node_gain, node_hat, node_scale).astype(
        jnp.bfloat16
    )
    node_second_grad = jnp.dot(node_act.T, node_raw_grad, preferred_element_type=jnp.float32)
    node_act_grad = jnp.dot(node_raw_grad, node_second.T, preferred_element_type=jnp.float32)
    node_pre_grad = (node_act_grad * node_sig * (1.0 + node_pre * (1.0 - node_sig))).astype(
        jnp.bfloat16
    )
    node_first_grad = jnp.dot(node_input.T, node_pre_grad, preferred_element_type=jnp.float32)
    node_input_grad = jnp.dot(node_pre_grad, node_first.T, preferred_element_type=jnp.float32)
    update_grad = edge_cot.astype(jnp.float32) + node_input_grad[:, width:][recv_ids]
    edge_gain_grad = jnp.sum(update_grad * edge_hat, axis=0)
    edge_raw_grad = normalize_back(update_grad * edge_gain, edge_hat, edge_scale).astype(
        jnp.bfloat16
    )
    edge_second_grad = jnp.dot(edge_act.T, edge_raw_grad, preferred_element_type=jnp.float32)
    edge_act_grad = jnp.dot(edge_raw_grad, edge_second.T, preferred_element_type=jnp.float32)
    edge_pre_grad = (edge_act_grad * edge_sig * (1.0 + edge_pre * (1.0 - edge_sig))).astype(
        jnp.bfloat16
    )
    edge_first_grad = jnp.dot(edge_input.T, edge_pre_grad, preferred_element_type=jnp.float32)
    edge_input_grad = jnp.dot(edge_pre_grad, edge_first.T, preferred_element_type=jnp.float32)
    edge_grad = (edge_cot.astype(jnp.float32) + edge_input_grad[:, :width]).astype(jnp.bfloat16)
    sent_grad = edge_input_grad[:, width : 2 * width]
    node_partial = (
        node_upstream
        + node_input_grad[:, :width]
        + jax.ops.segment_sum(
            edge_input_grad[:, 2 * width :], recv_ids, num_segments=nodes_in.shape[0]
        )
    )
    weight_terms = (
        edge_first_grad,
        edge_second_grad,
        node_first_grad,
        node_second_grad,
        edge_gain_grad,
        node_gain_grad,
    )
    return (edge_grad, sent_grad, node_partial, weight_terms)


def on_device(
    edge_latents,
    node_latents,
    edge_cotangent,
    node_cotangent,
    senders,
    receivers,
    send_rows,
    edge_first,
    edge_second,
    edge_gain,
    node_first,
    node_second,
    node_gain,
):
    patches = lax.axis_size("patch")
    own_nodes = node_latents[0]
    count = own_nodes.shape[0]
    width = own_nodes.shape[1]
    extended = with_halo(own_nodes, (("patch", 0),), RIM)
    outgoing = own_nodes[send_rows]
    incoming = lax.all_to_all(outgoing, "patch", split_axis=0, concat_axis=0, tiled=True)
    table = jnp.concatenate([extended, incoming.reshape(patches * FAR, width)], axis=0)
    edge_grad, sent_grad, node_partial, weight_terms = layer_backward(
        edge_latents[0],
        table[senders],
        own_nodes,
        receivers,
        edge_cotangent[0],
        node_cotangent[0],
        edge_first,
        edge_second,
        edge_gain,
        node_first,
        node_second,
        node_gain,
    )
    table_grad = jax.ops.segment_sum(sent_grad, senders, num_segments=table.shape[0])
    from_next = from_behind(table_grad[:RIM].astype(jnp.bfloat16), "patch", -1).astype(jnp.float32)
    from_prev = from_behind(
        table_grad[RIM + count : 2 * RIM + count].astype(jnp.bfloat16), "patch", 1
    ).astype(jnp.float32)
    far_grad = table_grad[2 * RIM + count :].reshape(patches, FAR, width)
    returned = lax.all_to_all(
        far_grad.astype(jnp.bfloat16), "patch", split_axis=0, concat_axis=0, tiled=True
    ).astype(far_grad.dtype)
    node_total = node_partial + table_grad[RIM : RIM + count]
    node_total = node_total + jnp.pad(from_prev, ((0, count - RIM), (0, 0)))
    node_total = node_total + jnp.pad(from_next, ((count - RIM, 0), (0, 0)))
    node_total = node_total + jax.ops.segment_sum(
        returned.reshape(patches * FAR, width), send_rows.reshape(-1), num_segments=count
    )
    summed = lax.psum(
        (
            weight_terms[0],
            weight_terms[1],
            weight_terms[2],
            weight_terms[3],
            weight_terms[4],
            weight_terms[5],
        ),
        ("patch", "sample"),
    )
    finals = tuple((term.astype(jnp.bfloat16) for term in summed))
    return (
        edge_grad[None],
        node_total.astype(jnp.bfloat16)[None],
        finals[0],
        finals[1],
        finals[2],
        finals[3],
        finals[4],
        finals[5],
    )


def solution(mesh):
    return jax.shard_map(
        on_device,
        mesh=mesh,
        in_specs=(
            P("sample", "patch", None),
            P("sample", "patch", None),
            P("sample", "patch", None),
            P("sample", "patch", None),
            P("patch"),
            P("patch"),
            P("patch", None),
            P(),
            P(),
            P(),
            P(),
            P(),
            P(),
        ),
        out_specs=(
            P("sample", "patch", None),
            P("sample", "patch", None),
            P(),
            P(),
            P(),
            P(),
            P(),
            P(),
        ),
        check_vma=False,
    )
```

profile of v0, /device:TPU:32, one launch (start us, length us, event | category | flops | bytes accessed | tf_op | source)
XLA Modules:
  0.0 275.9 jit_solution(2588927336006680791)
XLA Ops:
  0.7 0.8 compare_select_fusion.2
  1.7 2.2 gather_fusion
  3.9 0.8 reshape.83
  4.7 11.8 %all-to-all-start = ((bf16[64,4,512]{2,1,0:T(4,128)(2,1)}), bf16[64,4,512]{2,1,0:T(4,128)(2,1)S(1)}, u32[]{:S(2)}, u32[]{:S(2)}) async-start(bf16[64,4,512]{2,1,0:T(4,128)(2,1)} %reshape.83), calls=%async_computation | async-start | bytes 524288 | tf_op jit(solution)/shard_map/all_to_all | solution.py:141
  16.7 1.6 collective-permute-start.1
  18.4 0.6 reshape.140
  19.1 1.5 copy.25
  20.6 5.1 %gather_fusion.2 = bf16[1024,512]{1,0:T(8,128)(2,1)} fusion(bf16[256,512]{1,0:T(8,128)(2,1)S(1)} %bitcast.48, s32[1024]{0:T(1024)S(1)} %fusion.31), kind=kCustom, calls=%fused_computation.2 | custom fusion | bytes 2101248 | tf_op jit(solution)/shard_map/gather | solution.py:59
  25.7 2.8 %all-to-all-done = bf16[64,4,512]{2,1,0:T(4,128)(2,1)S(1)} async-done(((bf16[64,4,512]{2,1,0:T(4,128)(2,1)}), bf16[64,4,512]{2,1,0:T(4,128)(2,1)S(1)}, u32[]{:S(2)}, u32[]{:S(2)}) %all-to-all-start) | async-done | bytes 262176 | tf_op jit(solution)/shard_map/all_to_all | solution.py:141
  28.5 0.8 reshape.75
  29.3 1.0 pad_maximum_fusion.3
  30.3 5.1 %gather_fusion.1 = bf16[1024,512]{1,0:T(8,128)(2,1)} fusion(bf16[576,512]{1,0:T(8,128)(2,1)S(1)} %pad_maximum_fusion.3, s32[1024]{0:T(1024)S(1)} %fusion.30), kind=kCustom, calls=%fused_computation.1 | custom fusion | bytes 2101248 | tf_op jit(solution)/shard_map/gather | solution.py:145
  35.3 5.3 %multiply_convert_fusion.2 = (bf16[1024,512]{1,0:T(8,128)(2,1)S(1)}, f32[1024,512]{1,0:T(8,128)}) fusion(bf16[1536,512]{1,0:T(8,128)(2,1)S(1)} %copy-done, bf16[1024,512]{1,0:T(8,128)(2,1)} %gather_fusion.2, bf16[1024,512]{1,0:T(8,128)(2,1)} %gather_fusion.1, bf16[1024,512]{1,0:T(8,128)(2,1)} %bitcast.52), kind=kOutput, calls=%fused_computation.21 | convolution fusion | flops 1622671360 | bytes 7864320 | tf_op jit(solution)/shard_map/dot_general | solution.py:61
  40.6 0.8 fusion.41
  41.7 1.0 copy-done.2
  42.7 1.6 fusion.5
  44.3 2.9 %copy.27 = f32[1024,512]{1,0:T(8,128)} copy(f32[1024,512]{0,1:T(8,128)} %fusion.5) | data formatting | bytes 4194304 | tf_op jit(solution)/shard_map/mul | solution.py:66
  47.2 7.6 %scatter_custom_fusion = f32[256,512]{1,0:T(8,128)S(1)} fusion(s32[1024]{0:T(1024)S(1)} %copy-done.18, f32[1024,512]{1,0:T(8,128)} %copy.27, f32[]{:T(128)} %constant.10.clone.1), kind=kCustom, calls=%fused_computation.59 | custom fusion | flops 524288 | bytes 524800 | tf_op jit(solution)/shard_map/scatter-add | solution.py:67
  54.8 1.7 fusion.24
  56.6 0.4 fusion.42
  57.5 0.3 fusion.22
  57.8 0.5 fusion.9
  58.3 1.6 fusion.36
  59.9 0.5 fusion.43
  60.4 1.8 fusion.23
  62.2 4.9 %gather_fusion.3 = f32[1024,512]{1,0:T(8,128)} fusion(f32[256,512]{1,0:T(8,128)S(1)} %slice.63, s32[1024]{0:T(1024)S(1)} %fusion.31), kind=kCustom, calls=%fused_computation.3 | custom fusion | bytes 4198400 | tf_op jit(solution)/shard_map/gather | solution.py:88
  67.1 2.9 %copy.28 = f32[1024,512]{0,1:T(8,128)} copy(f32[1024,512]{1,0:T(8,128)} %gather_fusion.3) | data formatting | bytes 4194304 | tf_op jit(solution)/shard_map/gather | solution.py:88
  70.1 3.2 %multiply_reduce_fusion = (f32[512]{0:T(512)S(1)}, f32[1024]{0:T(1024)S(1)}, f32[1024]{0:T(1024)S(1)}) fusion(f32[1024,512]{0,1:T(8,128)} %copy-done.2, f32[1024]{0:T(1024)S(1)} %add_rsqrt_fusion, f32[1024]{0:T(1024)S(1)} %broadcast_multiply_fusion.2, f32[1024,512]{0,1:T(8,128)} %copy.28, bf16[1,1024,512]{1,2,0:T(8,128)(2,1)S(1)} %copy.25, f32[512]{0:T(512)S(1)} %copy-done.15), kind=kLoop, calls=%fused_computation.16 | loop fusion | flops 5240320 | bytes 5263360 | tf_op jit(solution)/shard_map/reduce_sum | solution.py:89
  73.5 0.7 multiply_convert_fusion.1
  74.2 0.5 copy-done.11
  74.8 1.7 fusion.45
  76.6 1.3 multiply_convert_fusion
  78.4 3.6 %fusion.6 = f32[1536,512]{1,0:T(8,128)} fusion(bf16[1024,512]{1,0:T(8,128)(2,1)S(1)} %multiply_convert_fusion, bf16[1024,512]{1,0:T(8,128)(2,1)S(1)} %copy-done.7, bf16[1024,512]{1,0:T(8,128)(2,1)S(1)} %copy-done.8, bf16[1024,512]{1,0:T(8,128)(2,1)S(1)} %bitcast.53), kind=kOutput, calls=%fused_computation.26 | convolution fusion | flops 1620049920 | bytes 7340032 | tf_op jit(solution)/shard_map/dot_general | solution.py:98
  82.0 4.5 %fusion.44 = f32[1024,1536]{1,0:T(8,128)} fusion(bf16[1024,512]{1,0:T(8,128)(2,1)S(1)} %multiply_convert_fusion, bf16[1536,512]{1,0:T(8,128)(2,1)S(1)} %copy-done), kind=kOutput, calls=%fused_computation.87 | convolution fusion | flops 1610612736 | bytes 8912896 | tf_op jit(solution)/shard_map/dot_general | solution.py:99
  86.5 8.4 %scatter_custom_fusion.1 = f32[576,512]{1,0:T(8,128)} fusion(s32[1024]{0:T(1024)S(1)} %copy-done.17, f32[1024,1536]{1,0:T(8,128)} %fusion.44, f32[]{:T(128)} %constant.10.clone.1), kind=kCustom, calls=%fused_computation.14 | custom fusion | flops 524288 | bytes 3277312 | tf_op jit(solution)/shard_map/scatter-add | solution.py:157
  94.9 1.3 convert.12
  96.3 3.1 %slice.64 = f32[1024,512]{1,0:T(8,128)} slice(f32[1024,1536]{1,0:T(8,128)} %fusion.44), slice={[0:1024], [0:512]} | slice | bytes 4194304 | tf_op jit(solution)/shard_map/slice | solution.py:100
  99.3 0.8 convert_element_type.83
  100.1 8.7 %all-to-all-start.1 = ((bf16[64,4,512]{2,1,0:T(4,128)(2,1)}), bf16[64,4,512]{2,1,0:T(4,128)(2,1)S(1)}, u32[]{:S(2)}, u32[]{:S(2)}) async-start(bf16[64,4,512]{2,1,0:T(4,128)(2,1)} %convert_element_type.83), calls=%async_computation.1 | async-start | bytes 524288 | tf_op jit(solution)/shard_map/all_to_all | solution.py:163
  109.1 1.6 collective-permute-start.3
  110.7 3.0 %copy.32 = f32[1024,512]{0,1:T(8,128)} copy(f32[1024,512]{1,0:T(8,128)} %slice.64) | data formatting | bytes 4194304
  113.7 144.9 %all-reduce.4 = (bf16[1536,512]{1,0:T(8,128)(2,1)}, bf16[512,512]{1,0:T(8,128)(2,1)}, bf16[1024,512]{1,0:T(8,128)(2,1)}, bf16[512,512]{1,0:T(8,128)(2,1)}, bf16[512]{0:T(512)(128)(2,1)}, /*index=5*/bf16[512]{0:T(512)(128)(2,1)}) all-reduce(f32[1536,512]{1,0:T(8,128)} %fusion.6, ...), channel_id=1, replica_groups=mesh['patch'=64,'sample'=4] {'patch','sample'}, use_global_device_ids=true, to_apply=%region_12.0 | all-reduce | flops 1836032 | bytes 11016192 | tf_op jit(solution)/shard_map/psum | solution.py:172
  258.6 2.9 %fusion.10 = bf16[1,1024,512]{1,2,0:T(8,128)(2,1)} fusion(f32[1024,512]{0,1:T(8,128)} %copy.32, bf16[1,1024,512]{1,2,0:T(8,128)(2,1)S(1)} %copy.25), kind=kLoop, calls=%fused_computation.31 | loop fusion | flops 1572864 | bytes 4194304 | tf_op jit(solution)/shard_map/broadcast_in_dim | solution.py:185
  261.5 2.4 copy.31
  263.9 1.2 fusion.21
  265.1 7.6 %scatter_custom_fusion.2 = f32[256,512]{1,0:T(8,128)S(1)} fusion(f32[256,512]{1,0:T(8,128)S(1)} %fusion.21, s32[1024]{0:T(1024)S(1)} %copy-done.18, f32[1024,1536]{1,0:T(8,128)} %fusion.44), kind=kCustom, calls=%fused_computation.12 | custom fusion | flops 524288 | bytes 2621440 | tf_op jit(solution)/shard_map/scatter-add | solution.py:105
  272.8 2.3 scatter_custom_fusion.3
  275.1 0.8 fusion.25
  (72 shorter events, 2.7 us)
Async XLA Ops:
  0.6 34.7 %copy-start = (bf16[1536,512]{1,0:T(8,128)(2,1)S(1)}, bf16[1536,512]{1,0:T(8,128)(2,1)}, u32[]{:S(2)}) copy-start(bf16[1536,512]{1,0:T(8,128)(2,1)} %param.20) | copy-start | bytes 4718596
  0.6 17.7 %copy-start.16 = (s32[64,4]{0,1:T(4,128)S(1)}, s32[64,4]{0,1:T(4,128)}, u32[]{:S(2)}) copy-start(s32[64,4]{0,1:T(4,128)} %param.19) | copy-start | bytes 3076
  0.7 15.8 %copy-start.1 = (bf16[1,256,512]{2,1,0:T(8,128)(2,1)S(1)}, bf16[1,256,512]{2,1,0:T(8,128)(2,1)}, u32[]{:S(2)}) copy-start(bf16[1,256,512]{2,1,0:T(8,128)(2,1)} %param.14) | copy-start | bytes 786436
  0.7 17.6 %copy-start.18 = (s32[1024]{0:T(1024)S(1)}, s32[1024]{0:T(1024)}, u32[]{:S(2)}) copy-start(s32[1024]{0:T(1024)} %param.18) | copy-start | bytes 12292
  0.7 17.6 %copy-start.17 = (s32[1024]{0:T(1024)S(1)}, s32[1024]{0:T(1024)}, u32[]{:S(2)}) copy-start(s32[1024]{0:T(1024)} %param.17) | copy-start | bytes 12292
  4.7 23.8 %all-to-all-start = ((bf16[64,4,512]{2,1,0:T(4,128)(2,1)}), bf16[64,4,512]{2,1,0:T(4,128)(2,1)S(1)}, u32[]{:S(2)}, u32[]{:S(2)}) async-start(bf16[64,4,512]{2,1,0:T(4,128)(2,1)} %reshape.83), calls=%async_computation | async-start | bytes 524288 | tf_op jit(solution)/shard_map/all_to_all | solution.py:141
  16.5 12.8 %collective-permute-start = (bf16[32,512]{1,0:T(8,128)(2,1)S(1)}, bf16[32,512]{1,0:T(8,128)(2,1)S(1)}, u32[]{:S(2)}, u32[]{:S(2)}) collective-permute-start(bf16[32,512]{1,0:T(8,128)(2,1)S(1)} %get-tuple-element.38), channel_id=1, source_target_pairs={{0,4},{4,8},{8,12},{12,16},{16,20},{20,24},{24,28},{28,32},{32,36}... | collective-permute-start | bytes 98312 | tf_op jit(solution)/shard_map/ppermute | solution.py:17
  16.7 12.6 %collective-permute-start.1 = (bf16[32,512]{1,0:T(8,128)(2,1)S(1)}, bf16[32,512]{1,0:T(8,128)(2,1)S(1)}, u32[]{:S(2)}, u32[]{:S(2)}) collective-permute-start(bf16[32,512]{1,0:T(8,128)(2,1)S(1)} %get-tuple-element.39), channel_id=1, source_target_pairs={{4,0},{8,4},{12,8},{16,12},{20,16},{24,20},{28,24},{32,28},{36,32}... | collective-permute-start | bytes 98312 | tf_op jit(solution)/shard_map/ppermute | solution.py:19
  35.3 5.3 %copy-start.13 = (bf16[512,512]{1,0:T(8,128)(2,1)S(1)}, bf16[512,512]{1,0:T(8,128)(2,1)}, u32[]{:S(2)}) copy-start(bf16[512,512]{1,0:T(8,128)(2,1)} %param.21) | copy-start | bytes 1572868
  40.6 1.1 copy-start.10
  40.6 2.1 copy-start.15
  41.4 1.3 copy-start.2
  54.8 1.8 copy-start.21
  56.5 1.0 copy-start.12
  56.6 0.9 copy-start.19
  58.3 1.6 copy-start.9
  60.4 1.8 copy-start.5
  70.1 3.2 %copy-start.3 = (f32[1024,512]{0,1:T(8,128)S(1)}, f32[1024,512]{0,1:T(8,128)}, u32[]{:S(2)}) copy-start(f32[1024,512]{0,1:T(8,128)} %copy-done.2) | copy-start | bytes 6291460
  70.1 3.5 %copy-start.4 = (f32[1024,512]{0,1:T(8,128)S(1)}, f32[1024,512]{0,1:T(8,128)}, u32[]{:S(2)}) copy-start(f32[1024,512]{0,1:T(8,128)} %copy.28) | copy-start | bytes 6291460
  73.5 1.2 copy-start.11
  74.8 1.8 copy-start.14
  74.8 1.8 copy-start.22
  76.6 1.3 copy-start.7
  76.6 1.5 copy-start.8
  76.6 1.9 copy-start.20
  100.1 172.6 %all-to-all-start.1 = ((bf16[64,4,512]{2,1,0:T(4,128)(2,1)}), bf16[64,4,512]{2,1,0:T(4,128)(2,1)S(1)}, u32[]{:S(2)}, u32[]{:S(2)}) async-start(bf16[64,4,512]{2,1,0:T(4,128)(2,1)} %convert_element_type.83), calls=%async_computation.1 | async-start | bytes 524288 | tf_op jit(solution)/shard_map/all_to_all | solution.py:163
  108.9 155.0 %collective-permute-start.2 = (bf16[32,512]{1,0:T(8,128)(2,1)S(1)}, bf16[32,512]{1,0:T(8,128)(2,1)S(1)}, u32[]{:S(2)}, u32[]{:S(2)}) collective-permute-start(bf16[32,512]{1,0:T(8,128)(2,1)S(1)} %get-tuple-element.36), channel_id=1, source_target_pairs={{0,4},{4,8},{8,12},{12,16},{16,20},{20,24},{24,28},{28,32},{32,36}... | collective-permute-start | bytes 98312 | tf_op jit(solution)/shard_map/ppermute | solution.py:28
  109.1 154.8 %collective-permute-start.3 = (bf16[32,512]{1,0:T(8,128)(2,1)S(1)}, bf16[32,512]{1,0:T(8,128)(2,1)S(1)}, u32[]{:S(2)}, u32[]{:S(2)}) collective-permute-start(bf16[32,512]{1,0:T(8,128)(2,1)S(1)} %get-tuple-element.37), channel_id=1, source_target_pairs={{0,252},{4,0},{8,4},{12,8},{16,12},{20,16},{24,20},{28,24},{32,28}... | collective-permute-start | bytes 98312 | tf_op jit(solution)/shard_map/ppermute | solution.py:28
  261.5 2.4 copy-start.6
where the time goes:
time: 277 us; the launch traced here: 276 us
  blocking collectives  145 us (52%)
  other arithmetic  40.4 us (15%)
  local copies, waits for them, and re-layouts  39 us (14%)
  starting transfers between devices  24.1 us (9%)
  matrix products  23.5 us (8%)
  waiting for transfers between devices  2.85 us (1%)
    psum x1, blocking collectives, on_device(): lax.psum((weight_terms[0], weight_terms[1], weight_terms[2], weight_terms...  145 us
    all_to_all x1, starting transfers between devices, on_device(): lax.all_to_all(outgoing, 'patch', split_axis=0, concat_axis=0, tiled=True)  11.8 us
    unnamed x50, local copies, waits for them, and re-layouts  9.6 us
    all_to_all x1, starting transfers between devices, on_device(): lax.all_to_all(far_grad.astype(jnp.bfloat16), 'patch', split_axis=0, conc...  8.74 us
    scatter-add x1, other arithmetic, on_device(): jax.ops.segment_sum(sent_grad, senders, num_segments=table.shape[0])  8.43 us
    gather x2, local copies, waits for them, and re-layouts, layer_backward(): node_input_grad[:, width:][recv_ids]  7.83 us
    scatter-add x1, other arithmetic, layer_backward(): jax.ops.segment_sum(edge_input_grad[:, 2 * width:], recv_ids, num_segment...  7.62 us
    scatter-add x1, other arithmetic, layer_backward(): jax.ops.segment_sum(update, recv_ids, num_segments=nodes_in.shape[0])  7.56 us
  transfers between devices with their start and end apart: 6, of which 1 were waited for; matrix products, arithmetic and copies ran while one was open for 9% of the time, Pallas kernels for 0%

commit v1 on v0

--- a/solution.py
+++ b/solution.py
@@ -169,17 +169,16 @@
     node_total = node_total + jax.ops.segment_sum(
         returned.reshape(patches * FAR, width), send_rows.reshape(-1), num_segments=count
     )
-    summed = lax.psum(
-        (
-            weight_terms[0],
-            weight_terms[1],
-            weight_terms[2],
-            weight_terms[3],
-            weight_terms[4],
-            weight_terms[5],
-        ),
-        ("patch", "sample"),
-    )
+    summed = (
+        weight_terms[0],
+        weight_terms[1],
+        weight_terms[2],
+        weight_terms[3],
+        weight_terms[4],
+        weight_terms[5],
+    )
+    for mesh_axis in ("patch", "sample"):
+        summed = lax.psum(summed, mesh_axis)
     finals = tuple((term.astype(jnp.bfloat16) for term in summed))
     return (
         edge_grad[None],

time: 277 us -> 435 us (1.57)
  blocking collectives: 145 us -> 257 us
  waiting for transfers between devices: 2.85 us -> 34.8 us
  between operations: 1.02 us -> 14.4 us
    psum x1 -> x2, blocking collectives: 145 us -> 257 us  [on_device(): summed = lax.psum(summed, mesh_axis)]
    psum x0 -> x1, waiting for transfers between devices: none -> 31.2 us  [on_device(): summed = lax.psum(summed, mesh_axis)]
    unnamed x50 -> x56, local copies, waits for them, and re-layouts: 9.6 us -> 10.6 us
  transfers between devices with their start and end apart: 6 -> 7, of which waited for: 1 -> 2; matrix products, arithmetic and copies ran while one was open for 9% -> 11% of each run, Pallas kernels for 0% -> 0%
where the time goes in v1:
time: 435 us; the launch traced here: 434 us
  blocking collectives  257 us (59%)
  local copies, waits for them, and re-layouts  40.2 us (9%)
  other arithmetic  39.3 us (9%)
  waiting for transfers between devices  34.8 us (8%)
  matrix products  24.7 us (6%)
  starting transfers between devices  23.4 us (5%)
  between operations  14.4 us (3%)
    psum x2, blocking collectives, on_device(): summed = lax.psum(summed, mesh_axis)  257 us
    psum x1, waiting for transfers between devices, on_device(): summed = lax.psum(summed, mesh_axis)  31.2 us
    all_to_all x1, starting transfers between devices, on_device(): lax.all_to_all(outgoing, 'patch', split_axis=0, concat_axis=0, tiled=True)  11.8 us
    unnamed x56, local copies, waits for them, and re-layouts  10.6 us
  transfers between devices with their start and end apart: 7, of which 2 were waited for; matrix products, arithmetic and copies ran while one was open for 11% of the time, Pallas kernels for 0%

profile of v1, /device:TPU:32, one launch (start us, length us, event | category | flops | bytes accessed | tf_op | source)
XLA Modules:
  0.0 433.9 jit_solution(17201882210306572581)
XLA Ops:
  7.2 0.8 compare_select_fusion.2
  8.2 2.2 gather_fusion
  10.4 0.8 reshape.83
  11.2 11.8 %all-to-all-start = ((bf16[64,4,512]{2,1,0:T(4,128)(2,1)}), bf16[64,4,512]{2,1,0:T(4,128)(2,1)S(1)}, u32[]{:S(2)}, u32[]{:S(2)}) async-start(bf16[64,4,512]{2,1,0:T(4,128)(2,1)} %reshape.83), calls=%async_computation | async-start | bytes 524288 | tf_op jit(solution)/shard_map/all_to_all | solution.py:141
  23.3 1.6 collective-permute-start.1
  24.9 1.5 copy.25
  26.4 5.1 %gather_fusion.2 = bf16[1024,512]{1,0:T(8,128)(2,1)} fusion(bf16[256,512]{1,0:T(8,128)(2,1)S(1)} %bitcast.48, s32[1024]{0:T(1024)S(1)} %fusion.31), kind=kCustom, calls=%fused_computation.2 | custom fusion | bytes 2101248 | tf_op jit(solution)/shard_map/gather | solution.py:59
  31.5 3.5 all-to-all-done
  35.0 0.8 reshape.75
  35.8 1.0 pad_maximum_fusion.3
  36.8 5.1 %gather_fusion.1 = bf16[1024,512]{1,0:T(8,128)(2,1)} fusion(bf16[576,512]{1,0:T(8,128)(2,1)S(1)} %pad_maximum_fusion.3, s32[1024]{0:T(1024)S(1)} %fusion.30), kind=kCustom, calls=%fused_computation.1 | custom fusion | bytes 2101248 | tf_op jit(solution)/shard_map/gather | solution.py:145
  41.9 5.3 %multiply_convert_fusion.2 = (bf16[1024,512]{1,0:T(8,128)(2,1)S(1)}, f32[1024,512]{1,0:T(8,128)}) fusion(bf16[1536,512]{1,0:T(8,128)(2,1)S(1)} %copy-done, bf16[1024,512]{1,0:T(8,128)(2,1)} %gather_fusion.2, bf16[1024,512]{1,0:T(8,128)(2,1)} %gather_fusion.1, bf16[1024,512]{1,0:T(8,128)(2,1)} %bitcast.52), kind=kOutput, calls=%fused_computation.21 | convolution fusion | flops 1622671360 | bytes 7864320 | tf_op jit(solution)/shard_map/dot_general | solution.py:61
  47.1 0.8 fusion.41
  48.3 1.0 copy-done.2
  49.2 1.6 fusion.5
  50.8 2.9 copy.27
  53.7 7.6 %scatter_custom_fusion = f32[256,512]{1,0:T(8,128)S(1)} fusion(s32[1024]{0:T(1024)S(1)} %copy-done.19, f32[1024,512]{1,0:T(8,128)} %copy.27, f32[]{:T(128)} %constant.10.clone.1), kind=kCustom, calls=%fused_computation.59 | custom fusion | flops 524288 | bytes 524800 | tf_op jit(solution)/shard_map/scatter-add | solution.py:67
  61.4 1.7 fusion.24
  64.4 0.5 fusion.9
  64.9 1.5 fusion.36
  66.9 1.8 fusion.23
  68.7 4.9 %gather_fusion.3 = f32[1024,512]{1,0:T(8,128)} fusion(f32[256,512]{1,0:T(8,128)S(1)} %slice.63, s32[1024]{0:T(1024)S(1)} %fusion.31), kind=kCustom, calls=%fused_computation.3 | custom fusion | bytes 4198400 | tf_op jit(solution)/shard_map/gather | solution.py:88
  73.7 2.9 copy.28
  76.6 3.2 multiply_reduce_fusion
  80.1 0.7 multiply_convert_fusion.1
  80.8 0.5 copy-done.12
  81.3 1.8 fusion.45
  83.1 1.3 multiply_convert_fusion
  84.4 1.0 copy-done.24
  85.4 3.5 fusion.6
  88.9 0.7 copy-done.17
  89.7 0.7 reshape.140
  90.3 5.7 %fusion.44 = f32[1024,1536]{1,0:T(8,128)} fusion(bf16[1024,512]{1,0:T(8,128)(2,1)} %copy-done.24, bf16[1536,512]{1,0:T(8,128)(2,1)S(1)} %copy-done), kind=kOutput, calls=%fused_computation.87 | convolution fusion | flops 1610612736 | bytes 8912896 | tf_op jit(solution)/shard_map/dot_general | solution.py:99
  96.0 8.4 %scatter_custom_fusion.1 = f32[576,512]{1,0:T(8,128)} fusion(s32[1024]{0:T(1024)S(1)} %copy-done.18, f32[1024,1536]{1,0:T(8,128)} %fusion.44, f32[]{:T(128)} %constant.10.clone.1), kind=kCustom, calls=%fused_computation.14 | custom fusion | flops 524288 | bytes 3277312 | tf_op jit(solution)/shard_map/scatter-add | solution.py:157
  104.5 3.2 slice.64
  107.8 0.8 convert_element_type.83
  108.6 8.0 %all-to-all-start.1 = ((bf16[64,4,512]{2,1,0:T(4,128)(2,1)}), bf16[64,4,512]{2,1,0:T(4,128)(2,1)S(1)}, u32[]{:S(2)}, u32[]{:S(2)}) async-start(bf16[64,4,512]{2,1,0:T(4,128)(2,1)} %convert_element_type.83), calls=%async_computation.1 | async-start | bytes 524288 | tf_op jit(solution)/shard_map/all_to_all | solution.py:163
  116.8 1.6 collective-permute-start.3
  118.4 2.9 copy.32
  121.3 2.9 fusion.10
  124.3 123.5 %all-reduce.2 = (f32[512]{0:T(512)S(1)}, f32[512]{0:T(512)}) all-reduce(f32[512]{0:T(512)S(1)} %get-tuple-element.24, f32[512]{0:T(512)S(1)} %get-tuple-element.27), channel_id=1, replica_groups=mesh['patch'=64,'sample'=4] {'patch'}, use_global_device_ids=true, to_apply=%region_21.22 | all-reduce | flops 1024 | bytes 8192 | tf_op jit(solution)/shard_map/psum | solution.py:181
  247.7 2.3 copy.31
  250.0 1.3 fusion.21
  251.3 7.7 %scatter_custom_fusion.2 = f32[256,512]{1,0:T(8,128)S(1)} fusion(f32[256,512]{1,0:T(8,128)S(1)} %fusion.21, s32[1024]{0:T(1024)S(1)} %copy-done.19, f32[1024,1536]{1,0:T(8,128)} %fusion.44), kind=kCustom, calls=%fused_computation.12 | custom fusion | flops 524288 | bytes 2621440 | tf_op jit(solution)/shard_map/scatter-add | solution.py:105
  259.0 2.3 scatter_custom_fusion.3
  261.4 0.8 fusion.25
  262.2 31.2 %all-reduce.8.cloned.1.call-done = (f32[1536,512]{1,0:T(8,128)}, f32[512,512]{1,0:T(8,128)}, f32[1024,512]{1,0:T(8,128)}, f32[512,512]{1,0:T(8,128)}) async-done(((f32[1536,512]{1,0:T(8,128)}, f32[512,512]{1,0:T(8,128)}, f32[1024,512]{1,0:T(8,128)}, f32[512,512]{1,0:T(8,128)}), (f32[1536,512]{1,0:T(8,128)}, f32[512,512]{1,0:T(8,128)}, f32[1024,512]{1,0:T(8,128)}, ...) | async-done | bytes 7340048 | tf_op jit(solution)/shard_map/psum | solution.py:181
  293.4 133.6 %all-reduce.9 = (bf16[1536,512]{1,0:T(8,128)(2,1)}, bf16[512,512]{1,0:T(8,128)(2,1)}, bf16[1024,512]{1,0:T(8,128)(2,1)}, bf16[512,512]{1,0:T(8,128)(2,1)}, bf16[512]{0:T(512)(128)(2,1)}, /*index=5*/bf16[512]{0:T(512)(128)(2,1)}) all-reduce(f32[1536,512]{1,0:T(8,128)} %get-tuple-element.32, ...), channel_id=1, replica_groups=mesh['patch'=64,'sample'=4] {'sample'}, use_global_device_ids=true, to_apply=%region_13.14 | all-reduce | flops 1836032 | bytes 11016192 | tf_op jit(solution)/shard_map/psum | solution.py:181
  (82 shorter events, 3.5 us)
Async XLA Ops:
  7.2 34.7 %copy-start = (bf16[1536,512]{1,0:T(8,128)(2,1)S(1)}, bf16[1536,512]{1,0:T(8,128)(2,1)}, u32[]{:S(2)}) copy-start(bf16[1536,512]{1,0:T(8,128)(2,1)} %param.20) | copy-start | bytes 4718596
  7.2 15.9 %copy-start.1 = (bf16[1,256,512]{2,1,0:T(8,128)(2,1)S(1)}, bf16[1,256,512]{2,1,0:T(8,128)(2,1)}, u32[]{:S(2)}) copy-start(bf16[1,256,512]{2,1,0:T(8,128)(2,1)} %param.14) | copy-start | bytes 786436
  7.2 17.7 %copy-start.19 = (s32[1024]{0:T(1024)S(1)}, s32[1024]{0:T(1024)}, u32[]{:S(2)}) copy-start(s32[1024]{0:T(1024)} %param.18) | copy-start | bytes 12292
  7.2 17.7 %copy-start.18 = (s32[1024]{0:T(1024)S(1)}, s32[1024]{0:T(1024)}, u32[]{:S(2)}) copy-start(s32[1024]{0:T(1024)} %param.17) | copy-start | bytes 12292
  11.2 23.8 %all-to-all-start = ((bf16[64,4,512]{2,1,0:T(4,128)(2,1)}), bf16[64,4,512]{2,1,0:T(4,128)(2,1)S(1)}, u32[]{:S(2)}, u32[]{:S(2)}) async-start(bf16[64,4,512]{2,1,0:T(4,128)(2,1)} %reshape.83), calls=%async_computation | async-start | bytes 524288 | tf_op jit(solution)/shard_map/all_to_all | solution.py:141
  23.0 270.4 %all-reduce.8.cloned.1.call-start = ((), (), s32[]{:S(2)}) async-start(), calls=%async_computation.2 | async-start | bytes 14680064 | tf_op jit(solution)/shard_map/psum | solution.py:181
  23.1 12.7 %collective-permute-start = (bf16[32,512]{1,0:T(8,128)(2,1)S(1)}, bf16[32,512]{1,0:T(8,128)(2,1)S(1)}, u32[]{:S(2)}, u32[]{:S(2)}) collective-permute-start(bf16[32,512]{1,0:T(8,128)(2,1)S(1)} %get-tuple-element.44), channel_id=1, source_target_pairs={{0,4},{4,8},{8,12},{12,16},{16,20},{20,24},{24,28},{28,32},{32,36}... | collective-permute-start | bytes 98312 | tf_op jit(solution)/shard_map/ppermute | solution.py:17
  23.3 12.5 %collective-permute-start.1 = (bf16[32,512]{1,0:T(8,128)(2,1)S(1)}, bf16[32,512]{1,0:T(8,128)(2,1)S(1)}, u32[]{:S(2)}, u32[]{:S(2)}) collective-permute-start(bf16[32,512]{1,0:T(8,128)(2,1)S(1)} %get-tuple-element.45), channel_id=1, source_target_pairs={{4,0},{8,4},{12,8},{16,12},{20,16},{24,20},{28,24},{32,28},{36,32}... | collective-permute-start | bytes 98312 | tf_op jit(solution)/shard_map/ppermute | solution.py:19
  41.9 5.3 %copy-start.14 = (bf16[512,512]{1,0:T(8,128)(2,1)S(1)}, bf16[512,512]{1,0:T(8,128)(2,1)}, u32[]{:S(2)}) copy-start(bf16[512,512]{1,0:T(8,128)(2,1)} %param.21) | copy-start | bytes 1572868
  47.1 1.1 copy-start.11
  47.1 2.1 copy-start.16
  47.9 1.3 copy-start.2
  61.3 1.8 copy-start.23
  63.1 1.0 copy-start.13
  63.1 0.9 copy-start.20
  64.8 1.6 copy-start.10
  66.9 1.8 copy-start.6
  76.6 3.2 copy-start.3
  76.6 3.5 copy-start.4
  80.1 1.2 copy-start.12
  81.3 1.8 copy-start.15
  81.3 1.8 copy-start.25
  83.1 2.3 copy-start.8
  83.1 2.3 copy-start.9
  83.1 2.3 copy-start.22
  84.4 1.0 copy-start.24
  88.9 0.7 copy-start.17
  104.5 3.2 copy-start.5
  108.6 150.4 %all-to-all-start.1 = ((bf16[64,4,512]{2,1,0:T(4,128)(2,1)}), bf16[64,4,512]{2,1,0:T(4,128)(2,1)S(1)}, u32[]{:S(2)}, u32[]{:S(2)}) async-start(bf16[64,4,512]{2,1,0:T(4,128)(2,1)} %convert_element_type.83), calls=%async_computation.1 | async-start | bytes 524288 | tf_op jit(solution)/shard_map/all_to_all | solution.py:163
  116.6 133.4 %collective-permute-start.2 = (bf16[32,512]{1,0:T(8,128)(2,1)S(1)}, bf16[32,512]{1,0:T(8,128)(2,1)S(1)}, u32[]{:S(2)}, u32[]{:S(2)}) collective-permute-start(bf16[32,512]{1,0:T(8,128)(2,1)S(1)} %get-tuple-element.42), channel_id=1, source_target_pairs={{0,4},{4,8},{8,12},{12,16},{16,20},{20,24},{24,28},{28,32},{32,36}... | collective-permute-start | bytes 98312 | tf_op jit(solution)/shard_map/ppermute | solution.py:28
  116.8 133.2 %collective-permute-start.3 = (bf16[32,512]{1,0:T(8,128)(2,1)S(1)}, bf16[32,512]{1,0:T(8,128)(2,1)S(1)}, u32[]{:S(2)}, u32[]{:S(2)}) collective-permute-start(bf16[32,512]{1,0:T(8,128)(2,1)S(1)} %get-tuple-element.43), channel_id=1, source_target_pairs={{0,252},{4,0},{8,4},{12,8},{16,12},{20,16},{24,20},{28,24},{32,28}... | collective-permute-start | bytes 98312 | tf_op jit(solution)/shard_map/ppermute | solution.py:28
  124.3 125.8 %copy-start.7 = (f32[256,1024]{1,0:T(8,128)S(1)}, f32[256,1024]{1,0:T(8,128)}, u32[]{:S(2)}) copy-start(f32[256,1024]{1,0:T(8,128)} %copy-done.6) | copy-start | bytes 3145732
  251.3 42.1 %copy-start.21 = (f32[512]{0:T(512)S(1)}, f32[512]{0:T(512)}, u32[]{:S(2)}) copy-start(f32[512]{0:T(512)} %get-tuple-element.31) | copy-start | bytes 6148
Sparse Core Ops, SparseCore 0:
  89.0 204.3 all-reduce.7
